TPU v7x, 512 devices: a whole 4x8x8 slice. The times are simulated.
512 devices in a mesh: user: 32 (over z_lo, x, core), item: 16 (over z_hi, y).
Axes of the slice: x: 4, y: 8, z: 8 (z_hi: 2, z_lo: 4; z = z_hi * 4 + z_lo), core: 2. Of those that a mesh axis runs over, the one named last changes fastest.
Arguments:
- user_x: bfloat16 [131072, 512], P(('user', 'item')), may hold values from -120 to 120
- item_x: bfloat16 [131072, 512], P(('user', 'item')), may hold values from -6 to 6
- lin_proj: bfloat16 [131072, 256], P(('user', 'item')), may hold values from -0.015625 to 0.015625
- tile_lists: int32 [512, 16], P('user'), may hold values from 0 to 2, as said below
- w_q: bfloat16 [512, 512], replicated, may hold values from -0.25 to 0.25
- w_k: bfloat16 [512, 512], replicated, may hold values from -0.25 to 0.25
- w_v: bfloat16 [512, 512], replicated, may hold values from -0.25 to 0.25
- w_o: bfloat16 [512, 512], replicated, may hold values from -1 to 1
- cotangent: bfloat16 [131072, 512], P(('user', 'item')), may hold values from -6 to 6
Outputs:
- updated: bfloat16 [131072, 512], P(('user', 'item'))
- user_grad: bfloat16 [131072, 512], P(('user', 'item'))
- item_grad: bfloat16 [131072, 512], P(('user', 'item'))
Inputs may be any that keep to these rules, and one draw needn't show every extreme that they name: `tile_lists`: A value below 2 names a tile of item device j of block b's group; 2 means no tile from it. Every block takes at least one tile, and in every group of 16 blocks some block takes a tile from every item device of the group.
All inputs are finite; a program needn't handle non-finite values.
Results may differ from a plain program's by a relative error of at most 0.009.
Values may be sent and summed in bfloat16 or wider, within the bound.
A program may use at most 128 MiB of HBM per device.

v0:
```python
import functools

import jax
import jax.numpy as jnp
from jax import lax
from jax.experimental import pallas as pl
from jax.experimental.pallas import tpu as pltpu
from jax.sharding import PartitionSpec as P

F32, BF16 = jnp.float32, jnp.bfloat16
HEADS, HEAD, WIDTH, TILE, RANK = 8, 64, 512, 128, 256
ROWS = 256
OWNERS = 16
KEYS = OWNERS * TILE + RANK
CHUNK = 256
CHUNKS = KEYS // CHUNK
VMEM_BYTES = 60 * 1024 * 1024
MESH = pl.DeviceIdType.MESH
ORDER = ((0, 1), (0, 2), (0, 3), (1, 1), (0, 0), (1, 2), None, (1, 3), (1, 0))
LINFORMER = 6


def dot(a, b):
    return lax.dot_general(a, b, (((1,), (0,)), ((), ())), preferred_element_type=F32)


def dot_t(a, b):
    return lax.dot_general(a, b, (((1,), (1,)), ((), ())), preferred_element_type=F32)


def split(a):
    high = a.astype(BF16)
    return high, (a - high.astype(F32)).astype(BF16)


class Place:
    def __init__(self):
        self.user, self.item = lax.axis_index("user"), lax.axis_index("item")
        self.near = lax.rem(self.user, 8)
        self.z_lo = lax.div(self.user, 8)
        self.y = lax.rem(self.item, 8)
        self.z_hi = lax.div(self.item, 8)
        self.z = self.z_hi * 4 + self.z_lo
        self.member = (self.near, self.z, self.y)

    def peer(self, group, k):
        if group == 0:
            return (self.z_lo * 8 + k, self.item)
        if group == 1:
            return (lax.rem(k, 4) * 8 + self.near, lax.div(k, 4) * 8 + self.y)
        return (self.user, self.z_hi * 8 + k)

    def along_y(self, step):
        return lax.rem(self.y + step + 8, 8)

    def partner(self):
        return (self.user, lax.rem(self.item + 8, 16))


def greet(place):
    barrier = pltpu.get_barrier_semaphore()
    for group in range(3):
        for r in range(1, 8):
            k = lax.rem(place.member[group] + r, 8)
            pl.semaphore_signal(barrier, inc=1, device_id=place.peer(group, k), device_id_type=MESH)
    pl.semaphore_wait(barrier, 21)


class Total:
    scratch = [
        pltpu.VMEM((8, 32, WIDTH), F32),
        pltpu.VMEM((8, 8, 256), F32),
        pltpu.VMEM((8, 8, 256), F32),
        pltpu.VMEM((8, 256), F32),
        pltpu.VMEM((8, 8, 256), F32),
        pltpu.VMEM((8, 256), F32),
        pltpu.VMEM((8, 8, 256), F32),
        pltpu.VMEM((32, WIDTH), F32),
        pltpu.SemaphoreType.DMA((5, 8)),
        pltpu.SemaphoreType.DMA((5, 8)),
    ]

    def __init__(self, place, part, out, scratch):
        self.place, self.part, self.out = place, part, out
        (self.land1, self.s1, self.land2, self.s2, self.land3, self.s3, self.land4, self.s4) = scratch[:8]
        self.send_sem, self.recv_sem = scratch[8:]

    def copies(self, phase):
        group = (0, 1, 2, 1, 0)[phase]
        land = (self.land1, self.land2, self.land3, self.land4, self.out)[phase]
        me = self.place.member[group]
        for r in range(1, 8):
            k = lax.rem(me + r, 8)
            source = (self.part.at[k], self.s1.at[k], self.s2, self.s3, self.s4)[phase]
            yield pltpu.make_async_remote_copy(
                src_ref=source,
                dst_ref=land.at[me],
                send_sem=self.send_sem.at[phase, r],
                recv_sem=self.recv_sem.at[phase, r],
                device_id=self.place.peer(group, k),
                device_id_type=MESH,
            )

    def start(self, phase):
        for copy in self.copies(phase):
            copy.start()

    def arrive(self, phase):
        for copy in self.copies(phase):
            copy.wait_recv()

    def step(self, phase):
        near, z, y = self.place.member
        if phase == 0:
            self.start(0)
            self.land1[near] = self.part[near]
            return
        self.arrive(phase - 1)
        if phase == 1:
            total = self.land1[0]
            for k in range(1, 8):
                total = total + self.land1[k]
            for p in range(8):
                self.s1[p] = total[p // 2 * 8 : p // 2 * 8 + 8, p % 2 * 256 : p % 2 * 256 + 256]
            self.start(1)
            self.land2[z] = self.s1[z]
        elif phase == 2:
            total = self.land2[0]
            for k in range(1, 8):
                total = total + self.land2[k]
            self.s2[...] = total
            self.start(2)
            self.land3[y] = total
        elif phase == 3:
            total = self.land3[0]
            for k in range(1, 8):
                total = total + self.land3[k]
            self.s3[...] = total
            self.start(3)
            self.land4[z] = total
        elif phase == 4:
            for p in range(8):
                self.s4[p // 2 * 8 : p // 2 * 8 + 8, p % 2 * 256 : p % 2 * 256 + 256] = self.land4[p]
            self.start(4)
            self.out[near] = self.s4[...]

    def finish(self):
        for phase in range(5):
            for copy in self.copies(phase):
                copy.wait_send()


class Attention:
    scratch = [
        pltpu.VMEM((CHUNKS, 4, CHUNK, 128), BF16),
        pltpu.VMEM((CHUNKS, 4, CHUNK, 128), BF16),
        pltpu.VMEM((CHUNKS, HEADS, HEAD, CHUNK), BF16),
        pltpu.VMEM((HEADS, HEAD, CHUNK), BF16),
        pltpu.VMEM((HEADS, 128, ROWS), BF16),
        pltpu.VMEM((HEADS, 128, ROWS), BF16),
        pltpu.VMEM((4, 2 * ROWS, 128), BF16),
        pltpu.VMEM((4, 2 * ROWS, 128), BF16),
        pltpu.VMEM((HEADS, HEAD, ROWS), F32),
        pltpu.VMEM((CHUNKS, HEADS, CHUNK, ROWS), F32),
        pltpu.VMEM((CHUNK, 2 * WIDTH), F32),
        pltpu.VMEM((HEADS, HEAD, ROWS), F32),
        pltpu.VMEM((HEADS, HEAD, ROWS), F32),
        pltpu.VMEM((HEADS, 1, ROWS), F32),
        pltpu.VMEM((HEADS, 1, ROWS), F32),
        pltpu.VMEM((HEADS, 1, ROWS), F32),
        pltpu.VMEM((CHUNKS, HEADS, 1, ROWS), F32),
        pltpu.VMEM((WIDTH, WIDTH), BF16),
        pltpu.VMEM((WIDTH, WIDTH), BF16),
    ]

    def __init__(self, weights, scratch):
        self.wq, self.wk, self.wv, self.wo = weights
        (self.k_s, self.v_s, self.kt_s, self.vt_s, self.qt_m, self.at_m, self.q_m, self.a_m, self.at_s,
         self.e_s, self.dkv, self.o_t, self.dq_t, self.top, self.den, self.delta, self.tops,
         self.wk_t, self.wv_t) = scratch

    def prepare(self, user_ref, cot_ref):
        q = dot(user_ref[...], self.wq[...]).astype(BF16).astype(F32) * (HEAD**-0.5)
        a = dot_t(cot_ref[...], self.wo[...]).astype(BF16).astype(F32)
        qt, at = q.T, a.T
        self.at_s[...] = at.reshape(HEADS, HEAD, ROWS)
        low_lane = lax.broadcasted_iota(jnp.int32, (ROWS, 128), 1) < HEAD
        low_row = lax.broadcasted_iota(jnp.int32, (128, ROWS), 0) < HEAD
        for p in range(4):
            cut = slice(p * 128, p * 128 + 128)
            for hh in range(2):
                lane, row = (low_lane, low_row) if hh == 0 else (~low_lane, ~low_row)
                half = slice(hh * ROWS, hh * ROWS + ROWS)
                self.q_m[p, half] = jnp.where(lane, q[:, cut], 0.0).astype(BF16)
                self.a_m[p, half] = jnp.where(lane, a[:, cut], 0.0).astype(BF16)
                self.qt_m[2 * p + hh] = jnp.where(row, qt[cut], 0.0).astype(BF16)
                self.at_m[2 * p + hh] = jnp.where(row, at[cut], 0.0).astype(BF16)
        self.wk_t[...] = self.wk[...].astype(F32).T.astype(BF16)
        self.wv_t[...] = self.wv[...].astype(F32).T.astype(BF16)
        self.top[...] = jnp.full(self.top.shape, -1e30, F32)
        self.den[...] = jnp.zeros(self.den.shape, F32)
        self.o_t[...] = jnp.zeros(self.o_t.shape, F32)
        self.dq_t[...] = jnp.zeros(self.dq_t.shape, F32)

    def keys(self, c, pieces):
        k = sum(dot(piece, self.wk[...]) for piece in pieces).astype(BF16)
        for p in range(4):
            self.k_s[c, p] = k[:, p * 128 : p * 128 + 128]
        v = sum(dot(piece, self.wv[...]) for piece in pieces).astype(BF16)
        for p in range(4):
            self.v_s[c, p] = v[:, p * 128 : p * 128 + 128]
        kt = sum(dot_t(self.wk_t[...], piece) for piece in pieces).astype(BF16)
        self.kt_s[c] = kt.reshape(HEADS, HEAD, CHUNK)
        vt = sum(dot_t(self.wv_t[...], piece) for piece in pieces).astype(BF16)
        self.vt_s[...] = vt.reshape(HEADS, HEAD, CHUNK)

    def forward(self, c, live):
        keep = [live[0] != 0, live[1] != 0]

        def score(h):
            return dot(self.k_s[c, h // 2], self.qt_m[h])

        s = score(0)
        for h in range(HEADS):
            following = score(h + 1) if h + 1 < HEADS else None
            s = jnp.concatenate(
                [jnp.where(keep[0], s[:TILE], -1e30), jnp.where(keep[1], s[TILE:], -1e30)], axis=0
            )
            before = self.top[h]
            top = jnp.maximum(before, jnp.max(s, axis=0, keepdims=True))
            e = jnp.exp(s - top)
            scale = jnp.exp(before - top)
            self.top[h] = top
            self.tops[c, h] = top
            self.e_s[c, h] = e
            self.den[h] = self.den[h] * scale + jnp.sum(e, axis=0, keepdims=True)
            self.o_t[h] = self.o_t[h] * scale + dot(self.vt_s[h], e.astype(BF16))
            s = following

    def settle(self):
        for h in range(HEADS):
            inverse = 1.0 / self.den[h]
            o = self.o_t[h] * inverse
            self.o_t[h] = o
            self.den[h] = inverse
            self.delta[h] = jnp.sum(o * self.at_s[h], axis=0, keepdims=True)

    def backward(self, c):
        def pull(p):
            return [dot(self.v_s[c, p], self.at_m[2 * p + hh]) for hh in range(2)]

        dp = pull(0)
        for p in range(4):
            following = pull(p + 1) if p < 3 else None
            ds, pb = [], []
            for hh in range(2):
                h = 2 * p + hh
                prob = self.e_s[c, h] * (jnp.exp(self.tops[c, h] - self.top[h]) * self.den[h])
                pb.append(prob.astype(BF16))
                ds.append((prob * (dp[hh] - self.delta[h])).astype(BF16))
                self.dq_t[h] = self.dq_t[h] + dot(self.kt_s[c, h], ds[hh])
            self.dkv[:, p * 128 : p * 128 + 128] = dot(jnp.concatenate(ds, axis=1), self.q_m[p])
            self.dkv[:, WIDTH + p * 128 : WIDTH + p * 128 + 128] = dot(jnp.concatenate(pb, axis=1), self.a_m[p])
            dp = following

    def to_items(self, piece):
        return dot_t(piece[:, :WIDTH], self.wk[...]) + dot_t(piece[:, WIDTH:], self.wv[...])

    def attended(self):
        return self.o_t[...].reshape(WIDTH, ROWS).T.astype(BF16)

    def d_query(self):
        return (self.dq_t[...] * (HEAD**-0.5)).reshape(WIDTH, ROWS).T.astype(BF16)


def ring_peer(place, way, hops=1):
    return place.z_hi * 8 + place.along_y(hops if way == 0 else -hops)


class Ring:
    semaphores = [
        pltpu.SemaphoreType.DMA((2, 2, 8)),
        pltpu.SemaphoreType.DMA((2, 2, 8)),
        pltpu.SemaphoreType.DMA((4,)),
        pltpu.SemaphoreType.DMA((4,)),
        pltpu.VMEM((2, TILE, WIDTH), BF16),
    ]

    def __init__(self, place, sems):
        self.place = place
        self.send_sem, self.recv_sem, self.zs, self.zr, self.relay_buf = sems

    def column(self, chain):
        return (self.place.z_hi if chain == 0 else 1 - self.place.z_hi) * 8

    def copy(self, chain, way, number):
        source, target = self.ends(chain, way, number)
        return pltpu.make_async_remote_copy(
            src_ref=source, dst_ref=target,
            send_sem=self.send_sem.at[chain, way, number], recv_sem=self.recv_sem.at[chain, way, number],
            device_id=(self.place.user, ring_peer(self.place, way)), device_id_type=MESH,
        )

    def push(self, chain, way, number):
        self.copy(chain, way, number).start()

    def wait(self, chain, way, number):
        self.copy(chain, way, number).wait_recv()

    def leap(self, number):
        tile = number % 2
        z = lax.rem(self.place.z + (2 if tile == 0 else 6), 8)
        near, far = self.cross_ends(tile)
        source, target = (near, self.relay_buf.at[tile]) if number < 2 else (self.relay_buf.at[tile], far)
        return pltpu.make_async_remote_copy(
            src_ref=source, dst_ref=target, send_sem=self.zs.at[number], recv_sem=self.zr.at[number],
            device_id=self.place.peer(1, z), device_id_type=MESH,
        )

    def cross(self, tile):
        self.leap(tile).start()

    def relay(self):
        for tile in range(2):
            self.leap(tile).wait_recv()
            self.leap(2 + tile).start()

    def wait_cross(self, tile):
        self.leap(2 + tile).wait_recv()

    def finish(self):
        for number in range(4):
            self.leap(number).wait_send()
        for chain in range(2):
            for way in range(2):
                for number in range(7):
                    self.copy(chain, way, number).wait_send()


def tile_rows(tile):
    return pl.ds(tile * TILE, TILE)


class Gather(Ring):
    scratch = [
        pltpu.VMEM((2, 2, TILE, WIDTH), BF16),
        pltpu.VMEM((2, 2, TILE // 2, WIDTH), BF16),
        pltpu.VMEM((2, 2, TILE, WIDTH), BF16),
        pltpu.VMEM((2, 2, TILE // 2, WIDTH), BF16),
        pltpu.VMEM((2, 2, TILE // 2, WIDTH), BF16),
    ] + Ring.semaphores

    def __init__(self, place, lists, x_ref, all_ref, scratch):
        self.lists, self.x, self.all = lists, x_ref, all_ref
        self.out3, self.out4, self.in3, self.via3, self.in4 = scratch[:5]
        super().__init__(place, scratch[5:])

    def source(self, chain, way, hops):
        return self.column(chain) + self.place.along_y(-hops if way == 0 else hops)

    def block(self, chain, index, own):
        return self.x if own and chain == 0 else self.all.at[index]

    def cross_ends(self, tile):
        z = lax.rem(self.place.z + (6 if tile == 0 else 2), 8)
        index = lax.div(z, 4) * 8 + self.place.y
        return self.x.at[tile_rows(tile)], self.all.at[index, tile_rows(tile)]

    def ends(self, chain, way, number):
        if number < 2:
            index = self.source(chain, way, 0)
            rows = tile_rows(number)
            return self.block(chain, index, True).at[rows], self.all.at[index, rows]
        if number < 4:
            part = self.all.at[self.source(chain, way, 1), tile_rows(number - 2)]
            return part, part
        source, target = {4: (self.out4, self.via3), 5: (self.out3, self.in3), 6: (self.via3, self.in4)}[number]
        return source.at[chain, way], target.at[chain, way]

    def first(self, chain, tile):
        for way in range(2):
            self.push(chain, way, tile)

    def second(self, chain):
        for tile in range(2):
            for way in range(2):
                self.wait(chain, way, tile)
                self.push(chain, way, 2 + tile)

    def third(self, chain):
        for way in range(2):
            index = self.source(chain, way, 2)
            for tile in range(2):
                self.wait(chain, way, 2 + tile)
            far = self.lists[ring_peer(self.place, way, 2), index] == 1
            low = way * (TILE // 2)
            self.out4[chain, way] = jnp.where(
                far,
                self.all[index, TILE + low : TILE + low + TILE // 2],
                self.all[index, low : low + TILE // 2],
            )
            self.push(chain, way, 4)
            near = self.lists[ring_peer(self.place, way, 1), index] == 1
            self.out3[chain, way] = jnp.where(near, self.all[index, TILE:], self.all[index, :TILE])
            self.push(chain, way, 5)

    def fourth(self, chain):
        for way in range(2):
            self.wait(chain, way, 4)
            self.push(chain, way, 6)

    def tiles(self, chain, e):
        found, live = [], []
        for way in ((1, 0) if e else (None, 4)):
            hops = 4 if way == 4 else e
            index = self.source(chain, 0 if way in (None, 4) else way, hops)
            tile = self.lists[self.place.item, index]
            live.append((tile < 2).astype(jnp.int32))
            if way == 4:
                for way in range(2):
                    self.wait(chain, way, 6)
                    found.append(self.in4[chain, way])
            elif e == 3:
                self.wait(chain, way, 5)
                found.append(self.in3[chain, way])
            else:
                block = self.block(chain, index, e == 0)
                found.append(jnp.where(tile == 1, block[TILE:], block[:TILE]))
        return jnp.concatenate(found, axis=0), live


class Scatter(Ring):
    scratch = [
        pltpu.VMEM((2, 2, TILE // 2, WIDTH), BF16),
        pltpu.VMEM((2, 2, TILE // 2, WIDTH), BF16),
        pltpu.VMEM((2, 2, TILE // 2, WIDTH), BF16),
        pltpu.VMEM((2, 2, TILE, WIDTH), BF16),
        pltpu.VMEM((2, 2, TILE, WIDTH), BF16),
        pltpu.VMEM((2, 2, 2, TILE, WIDTH), BF16),
        pltpu.VMEM((2, 2, 2, TILE, WIDTH), BF16),
        pltpu.VMEM((2, 2, 2, TILE, WIDTH), BF16),
        pltpu.VMEM((2, 2, 2, TILE, WIDTH), BF16),
        pltpu.VMEM((2, TILE, WIDTH), BF16),
        pltpu.VMEM((2, TILE, WIDTH), BF16),
        pltpu.VMEM((CHUNKS, CHUNK, WIDTH), F32),
    ] + Ring.semaphores

    def __init__(self, place, lists, scratch):
        self.lists = lists
        (self.out4, self.via3, self.in4, self.out3, self.in3, self.out2, self.in2, self.out1, self.in1,
         self.z_out, self.z_in, self.grads) = scratch[:12]
        super().__init__(place, scratch[12:])

    def owner(self, chain, way, hops):
        return self.column(chain) + self.place.along_y(hops if way == 0 else -hops)

    def cross_ends(self, tile):
        return self.z_out.at[tile], self.z_in.at[tile]

    def ends(self, chain, way, number):
        if number < 3:
            source, target = ((self.out4, self.via3), (self.via3, self.in4), (self.out3, self.in3))[number]
            return source.at[chain, way], target.at[chain, way]
        source, target = (self.out2, self.in2) if number < 5 else (self.out1, self.in1)
        tile = (number - 3) % 2
        return source.at[chain, way, tile], target.at[chain, way, tile]

    def own(self, chain, way, e):
        return self.grads[ORDER.index((chain, e)), tile_rows(0 if way == 0 else 1)]

    def lists_here(self, index, tile):
        return self.lists[self.place.item, index] == tile

    def send4(self, chain):
        for way in range(2):
            low = TILE + way * (TILE // 2)
            self.out4[chain, way] = self.grads[ORDER.index((chain, 0)), low : low + TILE // 2].astype(BF16)
            self.push(chain, way, 0)

    def send3(self, chain):
        for way in range(2):
            self.out3[chain, way] = self.own(chain, way, 3).astype(BF16)
            self.wait(chain, way, 0)
            self.push(chain, way, 1)
            self.push(chain, way, 2)

    def send2(self, chain):
        for way in range(2):
            index = self.owner(chain, way, 2)
            one, two = ring_peer(self.place, way, -1), ring_peer(self.place, way, -2)
            self.wait(chain, way, 1)
            self.wait(chain, way, 2)
            half = slice(way * (TILE // 2), way * (TILE // 2) + TILE // 2)
            other = slice((1 - way) * (TILE // 2), (1 - way) * (TILE // 2) + TILE // 2)
            for tile in range(2):
                value = jnp.where(self.lists_here(index, tile), self.own(chain, way, 2), 0.0)
                value = value + jnp.where(
                    self.lists[one, index] == tile, self.in3[chain, way].astype(F32), 0.0
                )
                far = jnp.where(self.lists[two, index] == tile, self.in4[chain, way].astype(F32), 0.0)
                self.out2[chain, way, tile, half] = (value[half] + far).astype(BF16)
                self.out2[chain, way, tile, other] = value[other].astype(BF16)
                self.push(chain, way, 3 + tile)

    def send1(self, chain):
        for tile in range(2):
            for way in range(2):
                index = self.owner(chain, way, 1)
                self.wait(chain, way, 3 + tile)
                value = jnp.where(self.lists_here(index, tile), self.own(chain, way, 1), 0.0)
                value = value + self.in2[chain, way, tile].astype(F32)
                self.out1[chain, way, tile] = value.astype(BF16)
                self.push(chain, way, 5 + tile)

    def total(self, chain, tile):
        for way in range(2):
            self.wait(chain, way, 5 + tile)
        value = jnp.where(self.lists_here(self.owner(chain, 0, 0), tile), self.own(chain, 0, 0), 0.0)
        return value + self.in1[chain, 0, tile].astype(F32) + self.in1[chain, 1, tile].astype(F32)

    def send_across(self):
        for tile in range(2):
            self.z_out[tile] = self.total(1, tile).astype(BF16)
            self.cross(tile)


def take(scratch, count):
    taken = scratch[:count]
    del scratch[:count]
    return taken


def kernel(
    lists_ref, user_ref, x_ref, proj_ref, wq_ref, wk_ref, wv_ref, wo_ref, cot_ref,
    att_ref, dq_ref, out_ref, all_x, part, lin_sum, lin_total, own_part, listed, live, *scratch
):
    scratch = list(scratch)
    place = Place()
    gather = Gather(place, lists_ref, x_ref, all_x, take(scratch, len(Gather.scratch)))
    scatter = Scatter(place, lists_ref, take(scratch, len(Scatter.scratch)))
    lin = Total(place, part, lin_sum, take(scratch, len(Total.scratch)))
    d_lin = Total(place, own_part, lin_total, take(scratch, len(Total.scratch)))
    attention = Attention((wq_ref, wk_ref, wv_ref, wo_ref), scratch)

    greet(place)
    for tile in range(2):
        gather.first(0, tile)
        gather.cross(tile)
    total = lax.dot_general(
        proj_ref[...], x_ref[...], (((0,), (0,)), ((), ())), preferred_element_type=F32
    )
    for k in range(8):
        part[k] = total[k * 32 : k * 32 + 32]
    lin.step(0)
    attention.prepare(user_ref, cot_ref)

    def before(i):
        if i == 0:
            gather.second(0)
            gather.relay()
        elif i == 1:
            lin.step(1)
            gather.third(0)
            for tile in range(2):
                gather.wait_cross(tile)
                gather.first(1, tile)
        elif i == 2:
            gather.fourth(0)
            lin.step(2)
        elif i == 3:
            lin.step(3)
            gather.second(1)
        elif i == 4:
            lin.step(4)
        elif i == 5:
            gather.third(1)
        elif i == 6:
            gather.fourth(1)
            lin.arrive(4)

    def forward_step(step, carry):
        for i, chunk in enumerate(ORDER):

            @pl.when(step == i)
            def _():
                before(i)
                if chunk is None:
                    live[0], live[1] = jnp.int32(1), jnp.int32(1)
                    attention.keys(i, split(lin_sum[...].reshape(RANK, WIDTH)))
                else:
                    rows, alive = gather.tiles(*chunk)
                    listed[...] = rows
                    live[0], live[1] = alive

        @pl.when(step != LINFORMER)
        def _():
            attention.keys(step, (listed[...],))

        attention.forward(step, live)
        return carry

    lax.fori_loop(0, CHUNKS, forward_step, 0)
    attention.settle()
    att_ref[...] = attention.attended()

    def after(i):
        if i == 8:
            scatter.send4(1)
        elif i == 7:
            scatter.send3(1)
        elif i == 6:
            d_lin.step(0)
        elif i == 5:
            scatter.send2(1)
        elif i == 4:
            scatter.send4(0)
            d_lin.step(1)
        elif i == 3:
            scatter.send1(1)
        elif i == 2:
            scatter.send3(0)
            d_lin.step(2)
        elif i == 1:
            scatter.send2(0)
            d_lin.step(3)

    def backward_step(step, carry):
        c = CHUNKS - 1 - step
        attention.backward(c)
        scatter.grads[c] = attention.to_items(attention.dkv[...].astype(BF16))
        for i in range(CHUNKS - 1, 0, -1):

            @pl.when(c == i)
            def _():
                if i == LINFORMER:
                    g = scatter.grads[i] + attention.to_items(split(attention.dkv[...])[1])
                    for k in range(8):
                        own_part[k] = g[k * 32 : k * 32 + 32]
                after(i)

        return carry

    lax.fori_loop(0, CHUNKS, backward_step, 0)
    scatter.send_across()
    d_lin.step(4)
    scatter.send1(0)
    dq_ref[...] = attention.d_query()
    scatter.relay()
    d_lin.arrive(4)
    back = jnp.zeros((ROWS, WIDTH), F32)
    for piece in split(lin_total[...].reshape(RANK, WIDTH)):
        back = back + dot(proj_ref[...], piece)
    for tile in range(2):
        value = back[tile * TILE : tile * TILE + TILE] + scatter.total(0, tile)
        scatter.wait_cross(tile)
        out_ref[tile * TILE : tile * TILE + TILE] = value + scatter.z_in[tile].astype(F32)
    lin.finish()
    d_lin.finish()
    gather.finish()
    scatter.finish()


def finish_kernel(att_ref, dq_ref, grad_ref, wq_ref, wo_ref, upd_ref, ug_ref, out_ref):
    upd_ref[...] = dot(att_ref[...], wo_ref[...]).astype(BF16)
    ug_ref[...] = dot_t(dq_ref[...], wq_ref[...]).astype(BF16)
    out_ref[...] = grad_ref[...].astype(BF16)


def in_vmem(count):
    return [pl.BlockSpec(memory_space=pltpu.VMEM)] * count


def per_device(user_x, item_x, lin_proj, tile_lists, w_q, w_k, w_v, w_o, cotangent):
    shape = jax.ShapeDtypeStruct
    sums = pltpu.VMEM((8, 32, WIDTH), F32)
    attended, d_query, grad = pl.pallas_call(
        kernel,
        out_shape=[shape((ROWS, WIDTH), BF16)] * 2 + [shape((ROWS, WIDTH), F32)],
        in_specs=[pl.BlockSpec(memory_space=pltpu.SMEM)] + in_vmem(8),
        out_specs=in_vmem(3),
        scratch_shapes=[
            pltpu.VMEM((OWNERS, ROWS, WIDTH), BF16),
            sums, sums, sums, sums,
            pltpu.VMEM((CHUNK, WIDTH), BF16),
            pltpu.SMEM((2,), jnp.int32),
        ] + Gather.scratch + Scatter.scratch + Total.scratch + Total.scratch + Attention.scratch,
        compiler_params=pltpu.CompilerParams(
            collective_id=0, has_side_effects=True, vmem_limit_bytes=VMEM_BYTES
        ),
        name="attend_and_exchange",
    )(tile_lists, user_x, item_x, lin_proj, w_q, w_k, w_v, w_o, cotangent)
    return pl.pallas_call(
        finish_kernel,
        out_shape=[shape((ROWS, WIDTH), BF16)] * 3,
        in_specs=in_vmem(5),
        out_specs=in_vmem(3),
        compiler_params=pltpu.CompilerParams(vmem_limit_bytes=VMEM_BYTES),
        name="finish",
    )(attended, d_query, grad, w_q, w_o)


def solution(mesh):
    rows = P(("user", "item"), None)
    return jax.shard_map(
        per_device,
        mesh=mesh,
        in_specs=(rows, rows, rows, P("user", None), P(), P(), P(), P(), rows),
        out_specs=(rows, rows, rows),
        check_vma=False,
    )
```

profile of v0, /device:TPU:1, one launch (start us, length us, event | category | flops | bytes accessed | tf_op | source)
XLA Modules:
  0.0 119.4 jit_solution(133029125376531134)
XLA Ops:
  0.6 116.0 %attend_and_exchange.1 = (bf16[256,512]{1,0:T(8,128)(2,1)}, bf16[256,512]{1,0:T(8,128)(2,1)}, f32[256,512]{1,0:T(8,128)}) custom-call(s32[16,16]{1,0:T(8,128)} %lists_ref.1, bf16[256,512]{1,0:T(8,128)(2,1)} %user_ref.1, bf16[256,512]{1,0:T(8,128)(2,1)} %x_ref.1, bf16[256,256]{1,0:T(8,128)(2,1)} %proj_ref.1, bf16[512,512]{1,0:T(8,128)(2,1)} %wq_ref.3, ...), custom_call_target="tpu_custom_call" | custom-call | tf_op jit(solution)/shard_map/attend_and_exchange/pallas_call | solution.py:676
  116.6 2.8 %finish.1 = (bf16[256,512]{1,0:T(8,128)(2,1)}, bf16[256,512]{1,0:T(8,128)(2,1)}, bf16[256,512]{1,0:T(8,128)(2,1)}) custom-call(bf16[256,512]{1,0:T(8,128)(2,1)} %get-tuple-element.6.att_ref, bf16[256,512]{1,0:T(8,128)(2,1)} %get-tuple-element.7.dq_ref, f32[256,512]{1,0:T(8,128)} %get-tuple-element.8.grad_ref, bf16[512,512]{1,0:T(8,128)(2,1)} %wq_ref.3, ...), custom_call_target="tpu_custom_call" | custom-call | tf_op jit(solution)/shard_map/finish/pallas_call | solution.py:692
where the time goes:
time: 120 us; the launch traced here: 119 us
  Pallas kernels  119 us (99%)
    pallas_call x1, Pallas kernels, per_device(): pl.pallas_call(kernel, out_shape=[shape((ROWS, WIDTH), BF16)] * 2 + [shap...  116 us
    pallas_call x1, Pallas kernels, per_device(): pl.pallas_call(finish_kernel, out_shape=[shape((ROWS, WIDTH), BF16)] * 3,...  2.75 us

commit v1 on v0

--- a/solution.py
+++ b/solution.py
@@ -16,8 +16,8 @@
 CHUNKS = KEYS // CHUNK
 VMEM_BYTES = 60 * 1024 * 1024
 MESH = pl.DeviceIdType.MESH
-ORDER = ((0, 1), (0, 2), (0, 3), (1, 1), (0, 0), (1, 2), None, (1, 3), (1, 0))
-LINFORMER = 6
+ORDER = ((0, 1), (0, 2), (1, 1), (0, 3), None, (1, 2), (0, 0), (1, 3), (1, 0))
+LINFORMER = 4
 
 
 def dot(a, b):
@@ -68,14 +68,14 @@
 
 class Total:
     scratch = [
-        pltpu.VMEM((8, 32, WIDTH), F32),
+        pltpu.VMEM((8, 32, WIDTH), BF16),
         pltpu.VMEM((8, 8, 256), F32),
         pltpu.VMEM((8, 8, 256), F32),
         pltpu.VMEM((8, 256), F32),
         pltpu.VMEM((8, 8, 256), F32),
         pltpu.VMEM((8, 256), F32),
         pltpu.VMEM((8, 8, 256), F32),
-        pltpu.VMEM((32, WIDTH), F32),
+        pltpu.VMEM((32, WIDTH), BF16),
         pltpu.SemaphoreType.DMA((5, 8)),
         pltpu.SemaphoreType.DMA((5, 8)),
     ]
@@ -117,9 +117,9 @@
             return
         self.arrive(phase - 1)
         if phase == 1:
-            total = self.land1[0]
+            total = self.land1[0].astype(F32)
             for k in range(1, 8):
-                total = total + self.land1[k]
+                total = total + self.land1[k].astype(F32)
             for p in range(8):
                 self.s1[p] = total[p // 2 * 8 : p // 2 * 8 + 8, p % 2 * 256 : p % 2 * 256 + 256]
             self.start(1)
@@ -139,8 +139,8 @@
             self.start(3)
             self.land4[z] = total
         elif phase == 4:
-            for p in range(8):
-                self.s4[p // 2 * 8 : p // 2 * 8 + 8, p % 2 * 256 : p % 2 * 256 + 256] = self.land4[p]
+            bands = [jnp.concatenate([self.land4[2 * p], self.land4[2 * p + 1]], axis=1) for p in range(4)]
+            self.s4[...] = jnp.concatenate(bands, axis=0).astype(BF16)
             self.start(4)
             self.out[near] = self.s4[...]
 
@@ -266,11 +266,13 @@
     def to_items(self, piece):
         return dot_t(piece[:, :WIDTH], self.wk[...]) + dot_t(piece[:, WIDTH:], self.wv[...])
 
-    def attended(self):
-        return self.o_t[...].reshape(WIDTH, ROWS).T.astype(BF16)
-
-    def d_query(self):
-        return (self.dq_t[...] * (HEAD**-0.5)).reshape(WIDTH, ROWS).T.astype(BF16)
+    def updated(self):
+        attended = self.o_t[...].reshape(WIDTH, ROWS).T.astype(BF16)
+        return dot(attended, self.wo[...]).astype(BF16)
+
+    def user_grad(self):
+        d_query = (self.dq_t[...] * (HEAD**-0.5)).reshape(WIDTH, ROWS).T.astype(BF16)
+        return dot_t(d_query, self.wq[...]).astype(BF16)
 
 
 def ring_peer(place, way, hops=1):
@@ -532,7 +534,7 @@
 
 def kernel(
     lists_ref, user_ref, x_ref, proj_ref, wq_ref, wk_ref, wv_ref, wo_ref, cot_ref,
-    att_ref, dq_ref, out_ref, all_x, part, lin_sum, lin_total, own_part, listed, live, *scratch
+    upd_ref, ug_ref, out_ref, all_x, part, lin_sum, lin_total, own_part, listed, live, *scratch
 ):
     scratch = list(scratch)
     place = Place()
@@ -550,7 +552,7 @@
         proj_ref[...], x_ref[...], (((0,), (0,)), ((), ())), preferred_element_type=F32
     )
     for k in range(8):
-        part[k] = total[k * 32 : k * 32 + 32]
+        part[k] = total[k * 32 : k * 32 + 32].astype(BF16)
     lin.step(0)
     attention.prepare(user_ref, cot_ref)
 
@@ -567,16 +569,16 @@
         elif i == 2:
             gather.fourth(0)
             lin.step(2)
-        elif i == 3:
             lin.step(3)
             gather.second(1)
+        elif i == 3:
+            lin.step(4)
         elif i == 4:
-            lin.step(4)
+            lin.arrive(4)
         elif i == 5:
             gather.third(1)
         elif i == 6:
             gather.fourth(1)
-            lin.arrive(4)
 
     def forward_step(step, carry):
         for i, chunk in enumerate(ORDER):
@@ -586,7 +588,7 @@
                 before(i)
                 if chunk is None:
                     live[0], live[1] = jnp.int32(1), jnp.int32(1)
-                    attention.keys(i, split(lin_sum[...].reshape(RANK, WIDTH)))
+                    attention.keys(i, (lin_sum[...].reshape(RANK, WIDTH),))
                 else:
                     rows, alive = gather.tiles(*chunk)
                     listed[...] = rows
@@ -601,7 +603,6 @@
 
     lax.fori_loop(0, CHUNKS, forward_step, 0)
     attention.settle()
-    att_ref[...] = attention.attended()
 
     def after(i):
         if i == 8:
@@ -609,20 +610,19 @@
         elif i == 7:
             scatter.send3(1)
         elif i == 6:
-            d_lin.step(0)
+            scatter.send4(0)
         elif i == 5:
             scatter.send2(1)
         elif i == 4:
-            scatter.send4(0)
+            d_lin.step(0)
+        elif i == 3:
+            scatter.send3(0)
+        elif i == 2:
+            scatter.send1(1)
             d_lin.step(1)
-        elif i == 3:
-            scatter.send1(1)
-        elif i == 2:
-            scatter.send3(0)
-            d_lin.step(2)
         elif i == 1:
             scatter.send2(0)
-            d_lin.step(3)
+            d_lin.step(2)
 
     def backward_step(step, carry):
         c = CHUNKS - 1 - step
@@ -635,35 +635,34 @@
                 if i == LINFORMER:
                     g = scatter.grads[i] + attention.to_items(split(attention.dkv[...])[1])
                     for k in range(8):
-                        own_part[k] = g[k * 32 : k * 32 + 32]
+                        own_part[k] = g[k * 32 : k * 32 + 32].astype(BF16)
                 after(i)
 
         return carry
 
     lax.fori_loop(0, CHUNKS, backward_step, 0)
     scatter.send_across()
+    d_lin.step(3)
+    upd_ref[...] = attention.updated()
+    ug_ref[...] = attention.user_grad()
+    scatter.send1(0)
+    scatter.relay()
     d_lin.step(4)
-    scatter.send1(0)
-    dq_ref[...] = attention.d_query()
-    scatter.relay()
     d_lin.arrive(4)
-    back = jnp.zeros((ROWS, WIDTH), F32)
-    for piece in split(lin_total[...].reshape(RANK, WIDTH)):
-        back = back + dot(proj_ref[...], piece)
+    back = dot(proj_ref[...], lin_total[...].reshape(RANK, WIDTH))
     for tile in range(2):
         value = back[tile * TILE : tile * TILE + TILE] + scatter.total(0, tile)
         scatter.wait_cross(tile)
-        out_ref[tile * TILE : tile * TILE + TILE] = value + scatter.z_in[tile].astype(F32)
+        out_ref[tile * TILE : tile * TILE + TILE] = (value + scatter.z_in[tile].astype(F32)).astype(BF16)
     lin.finish()
     d_lin.finish()
     gather.finish()
     scatter.finish()
 
 
-def finish_kernel(att_ref, dq_ref, grad_ref, wq_ref, wo_ref, upd_ref, ug_ref, out_ref):
-    upd_ref[...] = dot(att_ref[...], wo_ref[...]).astype(BF16)
-    ug_ref[...] = dot_t(dq_ref[...], wq_ref[...]).astype(BF16)
-    out_ref[...] = grad_ref[...].astype(BF16)
+def finish_kernel(*refs):
+    for k in range(3):
+        refs[3 + k][...] = refs[k][...]
 
 
 def in_vmem(count):
@@ -672,10 +671,10 @@
 
 def per_device(user_x, item_x, lin_proj, tile_lists, w_q, w_k, w_v, w_o, cotangent):
     shape = jax.ShapeDtypeStruct
-    sums = pltpu.VMEM((8, 32, WIDTH), F32)
-    attended, d_query, grad = pl.pallas_call(
+    sums = pltpu.VMEM((8, 32, WIDTH), BF16)
+    results = pl.pallas_call(
         kernel,
-        out_shape=[shape((ROWS, WIDTH), BF16)] * 2 + [shape((ROWS, WIDTH), F32)],
+        out_shape=[shape((ROWS, WIDTH), BF16)] * 3,
         in_specs=[pl.BlockSpec(memory_space=pltpu.SMEM)] + in_vmem(8),
         out_specs=in_vmem(3),
         scratch_shapes=[
@@ -692,11 +691,11 @@
     return pl.pallas_call(
         finish_kernel,
         out_shape=[shape((ROWS, WIDTH), BF16)] * 3,
-        in_specs=in_vmem(5),
+        in_specs=in_vmem(3),
         out_specs=in_vmem(3),
         compiler_params=pltpu.CompilerParams(vmem_limit_bytes=VMEM_BYTES),
         name="finish",
-    )(attended, d_query, grad, w_q, w_o)
+    )(*results)
 
 
 def solution(mesh):

time: 120 us -> 119 us (level)
  no operation moved by 1% of the time
where the time goes in v1:
time: 119 us
  Pallas kernels  118 us (99%)
    pallas_call x1, Pallas kernels, per_device(): pl.pallas_call(kernel, out_shape=[shape((ROWS, WIDTH), BF16)] * 3, in_spe...  116 us

profile of v1, /device:TPU:1, one launch (start us, length us, event | category | flops | bytes accessed | tf_op | source)
XLA Modules:
  0.0 119.1 jit_solution(14744916835376502696)
XLA Ops:
  0.6 116.5 %attend_and_exchange.1 = (bf16[256,512]{1,0:T(8,128)(2,1)}, bf16[256,512]{1,0:T(8,128)(2,1)}, bf16[256,512]{1,0:T(8,128)(2,1)}) custom-call(s32[16,16]{1,0:T(8,128)} %lists_ref.1, bf16[256,512]{1,0:T(8,128)(2,1)} %user_ref.1, bf16[256,512]{1,0:T(8,128)(2,1)} %x_ref.1, bf16[256,256]{1,0:T(8,128)(2,1)} %proj_ref.1, bf16[512,512]{1,0:T(8,128)(2,1)} %wq_ref.1, ...), custom_call_target="tpu_custom_call" | custom-call | tf_op jit(solution)/shard_map/attend_and_exchange/pallas_call | solution.py:675
  117.1 2.0 %finish.1 = (bf16[256,512]{1,0:T(8,128)(2,1)}, bf16[256,512]{1,0:T(8,128)(2,1)}, bf16[256,512]{1,0:T(8,128)(2,1)}) custom-call(bf16[256,512]{1,0:T(8,128)(2,1)} %get-tuple-element.6.refs_0_, bf16[256,512]{1,0:T(8,128)(2,1)} %get-tuple-element.7.refs_1_, bf16[256,512]{1,0:T(8,128)(2,1)} %get-tuple-element.8.refs_2_), custom_call_target="tpu_custom_call" | custom-call | tf_op jit(solution)/shard_map/finish/pallas_call | solution.py:691

commit v2 on v1

--- a/solution.py
+++ b/solution.py
@@ -18,6 +18,8 @@
 MESH = pl.DeviceIdType.MESH
 ORDER = ((0, 1), (0, 2), (1, 1), (0, 3), None, (1, 2), (0, 0), (1, 3), (1, 0))
 LINFORMER = 4
+FORWARD = ((0, 1), (0, 2), (0, 3), (0, 0), (1, 1), None, (1, 2), (1, 3), (1, 0))
+FORWARD_CODE = sum(ORDER.index(chunk) * CHUNKS**k for k, chunk in enumerate(FORWARD))
 
 
 def dot(a, b):
@@ -533,8 +535,8 @@
 
 
 def kernel(
-    lists_ref, user_ref, x_ref, proj_ref, wq_ref, wk_ref, wv_ref, wo_ref, cot_ref,
-    upd_ref, ug_ref, out_ref, all_x, part, lin_sum, lin_total, own_part, listed, live, *scratch
+    lists_ref, x_ref, proj_ref, user_hbm, cot_hbm, wq_hbm, wk_hbm, wv_hbm, wo_hbm, upd_hbm, ug_hbm, out_ref,
+    user_ref, cot_ref, wq_ref, wk_ref, wv_ref, wo_ref, upd_ref, ug_ref, local_sem, all_x, part, lin_sum, lin_total, own_part, listed, live, *scratch
 ):
     scratch = list(scratch)
     place = Place()
@@ -544,6 +546,17 @@
     d_lin = Total(place, own_part, lin_total, take(scratch, len(Total.scratch)))
     attention = Attention((wq_ref, wk_ref, wv_ref, wo_ref), scratch)
 
+    arriving = [
+        pltpu.make_async_copy(source, target, local_sem.at[k])
+        for k, (source, target) in enumerate(
+            (
+                (user_hbm, user_ref), (wq_hbm, wq_ref), (cot_hbm, cot_ref), (wo_hbm, wo_ref),
+                (wk_hbm, wk_ref), (wv_hbm, wv_ref),
+            )
+        )
+    ]
+    for copy in arriving:
+        copy.start()
     greet(place)
     for tile in range(2):
         gather.first(0, tile)
@@ -554,6 +567,8 @@
     for k in range(8):
         part[k] = total[k * 32 : k * 32 + 32].astype(BF16)
     lin.step(0)
+    for copy in arriving:
+        copy.wait()
     attention.prepare(user_ref, cot_ref)
 
     def before(i):
@@ -569,39 +584,38 @@
         elif i == 2:
             gather.fourth(0)
             lin.step(2)
+        elif i == 3:
             lin.step(3)
+        elif i == 4:
             gather.second(1)
-        elif i == 3:
             lin.step(4)
-        elif i == 4:
+        elif i == 5:
             lin.arrive(4)
-        elif i == 5:
+        elif i == 6:
             gather.third(1)
-        elif i == 6:
+        elif i == 7:
             gather.fourth(1)
 
-    def forward_step(step, carry):
-        for i, chunk in enumerate(ORDER):
+    def forward_step(step, code):
+        c = lax.rem(code, CHUNKS)
+        for i, chunk in enumerate(FORWARD):
 
             @pl.when(step == i)
             def _():
                 before(i)
                 if chunk is None:
                     live[0], live[1] = jnp.int32(1), jnp.int32(1)
-                    attention.keys(i, (lin_sum[...].reshape(RANK, WIDTH),))
+                    listed[...] = lin_sum[...].reshape(RANK, WIDTH)
                 else:
                     rows, alive = gather.tiles(*chunk)
                     listed[...] = rows
                     live[0], live[1] = alive
 
-        @pl.when(step != LINFORMER)
-        def _():
-            attention.keys(step, (listed[...],))
-
-        attention.forward(step, live)
-        return carry
-
-    lax.fori_loop(0, CHUNKS, forward_step, 0)
+        attention.keys(c, (listed[...],))
+        attention.forward(c, live)
+        return lax.div(code, CHUNKS)
+
+    lax.fori_loop(0, CHUNKS, forward_step, jnp.int32(FORWARD_CODE))
     attention.settle()
 
     def after(i):
@@ -645,6 +659,12 @@
     d_lin.step(3)
     upd_ref[...] = attention.updated()
     ug_ref[...] = attention.user_grad()
+    leaving = [
+        pltpu.make_async_copy(upd_ref, upd_hbm, local_sem.at[6]),
+        pltpu.make_async_copy(ug_ref, ug_hbm, local_sem.at[7]),
+    ]
+    for copy in leaving:
+        copy.start()
     scatter.send1(0)
     scatter.relay()
     d_lin.step(4)
@@ -654,6 +674,8 @@
         value = back[tile * TILE : tile * TILE + TILE] + scatter.total(0, tile)
         scatter.wait_cross(tile)
         out_ref[tile * TILE : tile * TILE + TILE] = (value + scatter.z_in[tile].astype(F32)).astype(BF16)
+    for copy in leaving:
+        copy.wait()
     lin.finish()
     d_lin.finish()
     gather.finish()
@@ -669,15 +691,22 @@
     return [pl.BlockSpec(memory_space=pltpu.VMEM)] * count
 
 
+def anywhere(count):
+    return [pl.BlockSpec(memory_space=pl.ANY)] * count
+
+
 def per_device(user_x, item_x, lin_proj, tile_lists, w_q, w_k, w_v, w_o, cotangent):
     shape = jax.ShapeDtypeStruct
     sums = pltpu.VMEM((8, 32, WIDTH), BF16)
+    users, weights = pltpu.VMEM((ROWS, WIDTH), BF16), pltpu.VMEM((WIDTH, WIDTH), BF16)
     results = pl.pallas_call(
         kernel,
         out_shape=[shape((ROWS, WIDTH), BF16)] * 3,
-        in_specs=[pl.BlockSpec(memory_space=pltpu.SMEM)] + in_vmem(8),
-        out_specs=in_vmem(3),
+        in_specs=[pl.BlockSpec(memory_space=pltpu.SMEM)] + in_vmem(2) + anywhere(6),
+        out_specs=anywhere(2) + in_vmem(1),
         scratch_shapes=[
+            users, users, weights, weights, weights, weights, users, users,
+            pltpu.SemaphoreType.DMA((8,)),
             pltpu.VMEM((OWNERS, ROWS, WIDTH), BF16),
             sums, sums, sums, sums,
             pltpu.VMEM((CHUNK, WIDTH), BF16),
@@ -687,7 +716,7 @@
             collective_id=0, has_side_effects=True, vmem_limit_bytes=VMEM_BYTES
         ),
         name="attend_and_exchange",
-    )(tile_lists, user_x, item_x, lin_proj, w_q, w_k, w_v, w_o, cotangent)
+    )(tile_lists, item_x, lin_proj, user_x, cotangent, w_q, w_k, w_v, w_o)
     return pl.pallas_call(
         finish_kernel,
         out_shape=[shape((ROWS, WIDTH), BF16)] * 3,

time: 119 us -> 119 us (level)
  no operation moved by 1% of the time
where the time goes in v2:
time: 119 us
  Pallas kernels  118 us (99%)
    pallas_call x1, Pallas kernels, per_device(): pl.pallas_call(kernel, out_shape=[shape((ROWS, WIDTH), BF16)] * 3, in_spe...  116 us

profile of v2, /device:TPU:1, one launch (start us, length us, event | category | flops | bytes accessed | tf_op | source)
XLA Modules:
  0.0 118.5 jit_solution(869828748497801200)
XLA Ops:
  0.6 115.9 %attend_and_exchange.1 = (bf16[256,512]{1,0:T(8,128)(2,1)}, bf16[256,512]{1,0:T(8,128)(2,1)}, bf16[256,512]{1,0:T(8,128)(2,1)}) custom-call(s32[16,16]{1,0:T(8,128)} %lists_ref.1, bf16[256,512]{1,0:T(8,128)(2,1)} %x_ref.1, bf16[256,256]{1,0:T(8,128)(2,1)} %proj_ref.1, bf16[256,512]{1,0:T(8,128)(2,1)} %user_hbm.1, bf16[256,512]{1,0:T(8,128)(2,1)} %cot_hbm.1, ...), custom_call_target="tpu_custom_call" | custom-call | tf_op jit(solution)/shard_map/attend_and_exchange/pallas_call | solution.py:702
  116.5 2.0 %finish.1 = (bf16[256,512]{1,0:T(8,128)(2,1)}, bf16[256,512]{1,0:T(8,128)(2,1)}, bf16[256,512]{1,0:T(8,128)(2,1)}) custom-call(bf16[256,512]{1,0:T(8,128)(2,1)} %get-tuple-element.6.refs_0_, bf16[256,512]{1,0:T(8,128)(2,1)} %get-tuple-element.7.refs_1_, bf16[256,512]{1,0:T(8,128)(2,1)} %get-tuple-element.8.refs_2_), custom_call_target="tpu_custom_call" | custom-call | tf_op jit(solution)/shard_map/finish/pallas_call | solution.py:720
